TPU v7x, 256 devices: a whole 4x4x8 slice. The times are simulated.
256 devices in a mesh: expert: 16 (over x_lo, y, core), hidden: 16 (over z, x_hi).
Axes of the slice: x: 4 (x_hi: 2, x_lo: 2; x = x_hi * 2 + x_lo), y: 4, z: 8, core: 2. Of those that a mesh axis runs over, the one named last changes fastest.
Arguments:
- tokens: bfloat16 [4096, 7168], P('expert', 'hidden'), may hold values from -6 to 6
- route_ids: int32 [4096, 2], P('expert'), may hold values from 0 to 15, all different within a row; in each aligned block of 256 rows (0 to 255, 256 to 511, ...) at most 40 rows name the same one
- route_weight: float32 [4096, 2], P('expert'), may hold values from 0.2 to 2
- w_gate: bfloat16 [16, 7168, 2048], P('expert', None, 'hidden'), may hold values from -0.0625 to 0.0625
- w_up: bfloat16 [16, 7168, 2048], P('expert', None, 'hidden'), may hold values from -0.0625 to 0.0625
- w_down: bfloat16 [16, 2048, 7168], P('expert', 'hidden'), may hold values from -0.125 to 0.125
Outputs:
- mixed: bfloat16 [4096, 7168], P('expert', 'hidden')
Inputs may be any that keep to these rules, and one draw needn't show every extreme that they name: `route_ids`: each row names 2 different experts. In the aligned blocks of 256 rows, no expert is named by more than 40 rows of one block, a bound that some block reaches.
All inputs are finite; a program needn't handle non-finite values.
Results may differ from a plain program's by a relative error of at most 0.0057.
Values may be sent and summed in bfloat16 or wider, within the bound.
No kernel may reach another device: no remote copies, remote signals or barrier semaphores. Data moves between devices by JAX's collectives and lax.ppermute only.
A program may use at most 128 MiB of HBM per device.

v0:
```python
import jax
import jax.numpy as jnp
from jax import lax
from jax.sharding import PartitionSpec as P

TOP = 2


def on_device(tokens, route_ids, route_weight, w_gate, w_up, w_down):
    experts = lax.axis_size("expert")
    rows_dev = tokens.shape[0]
    capacity = (rows_dev * TOP * 5 + 4 * experts - 1) // (4 * experts)
    slot_count = experts * capacity
    matches = route_ids[:, :, None] == jnp.arange(experts, dtype=jnp.int32)[None, None, :]
    chosen = jnp.sum(matches.astype(jnp.int32), axis=1)
    ranking = jnp.cumsum(chosen, axis=0) - chosen
    slot_ids = jnp.arange(capacity, dtype=jnp.int32)
    placed = (chosen.T[:, None, :] == 1) & (ranking.T[:, None, :] == slot_ids[None, :, None])
    every_row = lax.all_gather(tokens, "expert", axis=0, tiled=True)
    every_route = lax.all_gather(route_ids, "expert", axis=0, tiled=True)
    own_expert = lax.axis_index("expert")
    flagged = jnp.sum((every_route == own_expert).astype(jnp.int32), axis=1).reshape(
        experts, rows_dev
    )
    ordering = jnp.cumsum(flagged, axis=1) - flagged
    picks = (flagged[:, None, :] == 1) & (ordering[:, None, :] == slot_ids[None, :, None])
    arrived = jnp.einsum(
        "sct,std->scd",
        picks.astype(jnp.bfloat16),
        every_row.reshape(experts, rows_dev, -1),
        preferred_element_type=jnp.float32,
    ).astype(jnp.bfloat16)
    flat_rows = arrived.reshape(slot_count, -1)
    gate_w = w_gate[0]
    up_w = w_up[0]
    down_w = w_down[0]
    fragment = lax.all_gather(flat_rows, "hidden", axis=1, tiled=True)
    gate_sum = jnp.dot(fragment, gate_w, preferred_element_type=jnp.float32)
    up_sum = jnp.dot(fragment, up_w, preferred_element_type=jnp.float32)
    hidden = (jax.nn.silu(gate_sum) * up_sum).astype(jnp.bfloat16)
    partials = jnp.dot(hidden, down_w, preferred_element_type=jnp.float32)
    produced = lax.psum_scatter(partials, "hidden", scatter_dimension=1, tiled=True)
    produced = produced.astype(jnp.bfloat16).reshape(experts, capacity, -1)
    returned = lax.all_to_all(produced, "expert", split_axis=0, concat_axis=0, tiled=True)
    per_expert = jnp.sum(jnp.where(matches, route_weight[:, :, None], jnp.float32(0.0)), axis=1)
    combine_table = placed.astype(jnp.float32) * per_expert.T[:, None, :]
    mixed = jnp.einsum(
        "ect,ecd->td", combine_table, returned.astype(jnp.float32), precision=lax.Precision.HIGHEST
    )
    return mixed.astype(jnp.bfloat16)


def solution(mesh):
    in_specs = (
        P("expert", "hidden"),
        P("expert", None),
        P("expert", None),
        P("expert", None, "hidden"),
        P("expert", None, "hidden"),
        P("expert", "hidden", None),
    )
    out_specs = P("expert", "hidden")
    return jax.shard_map(
        on_device, mesh=mesh, in_specs=in_specs, out_specs=out_specs, check_vma=False
    )
```

profile of v0, /device:TPU:1, one launch (start us, length us, event | category | flops | bytes accessed | tf_op | source)
XLA Modules:
  0.0 564.6 jit_solution(8759587761792712818)
XLA Ops:
  6.5 0.0 copy-start
  6.5 0.0 all-gather.3.cloned.1.call-start
  6.5 0.7 all-gather.3.cloned.1.call-update
  7.3 0.0 all-gather.5.cloned.1.call-start
  7.3 21.5 %all_gather.9 = s32[4096,2]{0,1:T(2,128)S(1)} all-gather(s32[256,2]{0,1:T(2,128)} %param.7), channel_id=1, replica_groups=mesh['expert'=16,'hidden'=16] {'expert'}, dimensions={0}, use_global_device_ids=true | all-gather | bytes 34816 | tf_op jit(solution)/shard_map/all_gather | solution.py:20
  28.9 0.6 reduce-window.16
  29.5 0.2 slice_reduce_fusion
  29.7 0.1 bitcast_subtract_fusion
  29.8 30.3 %all-gather.3.cloned.1.call-done = bf16[4096,448]{0,1:T(8,128)(2,1)} async-done(((bf16[256,448]{0,1:T(8,128)(2,1)}), bf16[4096,448]{0,1:T(8,128)(2,1)}) %all-gather.3.cloned.1.call-update) | async-done | bytes 3670032 | tf_op jit(solution)/shard_map/all_gather | solution.py:19
  60.1 3.2 fusion.9
  63.3 1.1 copy.32
  64.4 0.0 all-gather.5.cloned.1.call-update
  64.4 0.0 reduce-scatter.2.cloned.1.call-start
  64.4 142.2 %all-gather.5.cloned.1.call-done = bf16[640,7168]{0,1:T(8,128)(2,1)} async-done(((bf16[640,448]{0,1:T(8,128)(2,1)}), bf16[640,7168]{0,1:T(8,128)(2,1)}) %all-gather.5.cloned.1.call-update) | async-done | bytes 9175056 | tf_op jit(solution)/shard_map/all_gather | solution.py:37
  206.6 6.7 %fusion.7 = f32[640,128]{1,0:T(8,128)S(1)} fusion(bf16[640,7168]{0,1:T(8,128)(2,1)} %all-gather.5.cloned.1.call-done, bf16[1,7168,128]{2,1,0:T(8,128)(2,1)} %param.9), kind=kOutput, calls=%fused_computation.7 | convolution fusion | flops 1174405120 | bytes 11337728 | tf_op jit(solution)/shard_map/dot_general | solution.py:38
  213.3 0.0 copy-done
  213.3 20.0 %fusion.3 = f32[640,7168]{0,1:T(8,128)} fusion(bf16[1,128,7168]{2,1,0:T(8,128)(2,1)S(1)} %copy-done, bf16[640,7168]{0,1:T(8,128)(2,1)} %all-gather.5.cloned.1.call-done, bf16[1,7168,128]{2,1,0:T(8,128)(2,1)} %param.10, f32[640,128]{1,0:T(8,128)S(1)} %fusion.7), kind=kOutput, calls=%fused_computation.3 | convolution fusion | flops 2349301760 | bytes 31522816 | tf_op jit(solution)/shard_map/dot_general | solution.py:41
  233.4 0.0 copy-start.1
  233.4 0.0 reduce-scatter.2.cloned.1.call-update
  233.4 0.7 copy-done.1
  234.0 0.0 copy-start.2
  234.1 0.6 reduce-window.14
  234.6 0.2 slice_reduce_fusion.1
  234.9 302.3 %reduce-scatter.2.cloned.1.call-done = f32[640,448]{0,1:T(8,128)} async-done(((f32[640,7168]{0,1:T(8,128)}), f32[640,448]{0,1:T(8,128)}) %reduce-scatter.2.cloned.1.call-update) | async-done | bytes 1146896 | tf_op jit(solution)/shard_map/reduce_scatter | solution.py:42
  537.1 1.3 convert_element_type.25
  538.5 1.1 copy.33
  539.6 5.5 all-to-all-start
  545.1 0.0 copy-done.2
  545.1 0.1 bitcast_subtract_fusion.1
  545.2 11.1 %all-to-all-done = bf16[16,40,448]{2,1,0:T(8,128)(2,1)S(1)} async-done(((bf16[16,40,448]{2,1,0:T(8,128)(2,1)}), bf16[16,40,448]{2,1,0:T(8,128)(2,1)S(1)}, u32[]{:S(2)}, u32[]{:S(2)}) %all-to-all-start) | async-done | bytes 573472 | tf_op jit(solution)/shard_map/all_to_all | solution.py:44
  556.4 1.7 fusion.12
  (12 shorter events, 0.2 us)
Async XLA Ops:
  6.5 206.8 %copy-start = (bf16[1,128,7168]{2,1,0:T(8,128)(2,1)S(1)}, bf16[1,128,7168]{2,1,0:T(8,128)(2,1)}, u32[]{:S(2)}) copy-start(bf16[1,128,7168]{2,1,0:T(8,128)(2,1)} %param.11) | copy-start | bytes 5505028
  6.5 53.6 %all-gather.3.cloned.1.call-start = ((), (), s32[]{:S(2)}) async-start(), calls=%async_computation.2 | async-start | bytes 3899392 | tf_op jit(solution)/shard_map/all_gather | solution.py:19
  7.3 199.4 %all-gather.5.cloned.1.call-start = ((), (), s32[]{:S(2)}) async-start(), calls=%async_computation.3 | async-start | bytes 9748480 | tf_op jit(solution)/shard_map/all_gather | solution.py:37
  64.4 472.8 %reduce-scatter.2.cloned.1.call-start = ((), (), s32[]{:S(2)}) async-start(), calls=%async_computation.4 | async-start | bytes 19496960 | tf_op jit(solution)/shard_map/reduce_scatter | solution.py:42
  233.4 0.7 copy-start.1
  234.0 311.1 %copy-start.2 = (f32[256,2]{0,1:T(2,128)S(1)}, f32[256,2]{0,1:T(2,128)}, u32[]{:S(2)}) copy-start(f32[256,2]{0,1:T(2,128)} %param.8) | copy-start | bytes 6148
  539.6 16.8 %all-to-all-start = ((bf16[16,40,448]{2,1,0:T(8,128)(2,1)}), bf16[16,40,448]{2,1,0:T(8,128)(2,1)S(1)}, u32[]{:S(2)}, u32[]{:S(2)}) async-start(bf16[16,40,448]{2,1,0:T(8,128)(2,1)} %bitcast.7), calls=%async_computation.1 | async-start | bytes 1310720 | tf_op jit(solution)/shard_map/all_to_all | solution.py:44
Sparse Core Ops, SparseCore 0:
  9.1 50.9 all-gather.2
  64.5 142.0 all-gather.4
  233.5 303.5 reduce-scatter.1
where the time goes:
time: 565 us
  waiting for transfers between devices  487 us (86%)
  matrix products  31.6 us (6%)
  blocking collectives  21.5 us (4%)
  between operations  13.2 us (2%)
    reduce_scatter x1, waiting for transfers between devices, on_device(): lax.psum_scatter(partials, 'hidden', scatter_dimension=1, tiled=True)  302 us
    all_gather x1, waiting for transfers between devices, on_device(): fragment = lax.all_gather(flat_rows, 'hidden', axis=1, tiled=True)  142 us
    all_gather x1, waiting for transfers between devices, on_device(): every_row = lax.all_gather(tokens, 'expert', axis=0, tiled=True)  30.3 us
    all_gather x1, blocking collectives, on_device(): every_route = lax.all_gather(route_ids, 'expert', axis=0, tiled=True)  21.5 us
    dot_general x1, matrix products, on_device(): partials = jnp.dot(hidden, down_w, preferred_element_type=jnp.float32)  20 us
  transfers between devices with their start and end apart: 4, of which 4 were waited for; matrix products, arithmetic and copies ran while one was open for 0% of the time, Pallas kernels for 0%

commit v1 on v0

--- a/solution.py
+++ b/solution.py
@@ -16,7 +16,9 @@
     ranking = jnp.cumsum(chosen, axis=0) - chosen
     slot_ids = jnp.arange(capacity, dtype=jnp.int32)
     placed = (chosen.T[:, None, :] == 1) & (ranking.T[:, None, :] == slot_ids[None, :, None])
-    every_row = lax.all_gather(tokens, "expert", axis=0, tiled=True)
+    every_row = jnp.concatenate(
+        lax.all_to_all(jnp.stack([tokens] * lax.axis_size("expert")), "expert", 0, 0), axis=0
+    )
     every_route = lax.all_gather(route_ids, "expert", axis=0, tiled=True)
     own_expert = lax.axis_index("expert")
     flagged = jnp.sum((every_route == own_expert).astype(jnp.int32), axis=1).reshape(

time: 565 us -> 587 us (1.039)
  blocking collectives: 21.5 us -> 62.3 us
  waiting for transfers between devices: 487 us -> 457 us
  starting transfers between devices: 5.63 us -> 13.2 us
    all_gather x1, blocking collectives: 21.5 us -> 62.3 us  [on_device(): every_route = lax.all_gather(route_ids, 'expert', axis=0, tiled=True)]
    all_gather x1 -> x0, waiting for transfers between devices: 30.3 us -> none  [on_device(): every_row = lax.all_gather(tokens, 'expert', axis=0, tiled=True)]
    all_to_all x0 -> x1, starting transfers between devices: none -> 7.6 us  [on_device(): lax.all_to_all(jnp.stack([tokens] * lax.axis_size('expert')), 'expert', 0...]
  transfers between devices with their start and end apart: 4 -> 4, of which waited for: 4 -> 3; matrix products, arithmetic and copies ran while one was open for 0% -> 0% of each run, Pallas kernels for 0% -> 0%
where the time goes in v1:
time: 587 us; the launch traced here: 586 us
  waiting for transfers between devices  457 us (78%)
  blocking collectives  62.3 us (11%)
  matrix products  31.6 us (5%)
  between operations  13.5 us (2%)
  starting transfers between devices  13.2 us (2%)
    reduce_scatter x1, waiting for transfers between devices, on_device(): lax.psum_scatter(partials, 'hidden', scatter_dimension=1, tiled=True)  303 us
    all_gather x1, waiting for transfers between devices, on_device(): fragment = lax.all_gather(flat_rows, 'hidden', axis=1, tiled=True)  143 us
    all_gather x1, blocking collectives, on_device(): every_route = lax.all_gather(route_ids, 'expert', axis=0, tiled=True)  62.3 us
    dot_general x1, matrix products, on_device(): partials = jnp.dot(hidden, down_w, preferred_element_type=jnp.float32)  20 us
  transfers between devices with their start and end apart: 4, of which 3 were waited for; matrix products, arithmetic and copies ran while one was open for 0% of the time, Pallas kernels for 0%

profile of v1, /device:TPU:1, one launch (start us, length us, event | category | flops | bytes accessed | tf_op | source)
XLA Modules:
  0.0 586.2 jit_solution(5995481655962362099)
XLA Ops:
  6.5 0.0 copy-start
  6.5 3.3 stack.2
  9.8 0.0 copy-start.1
  9.8 7.6 %all-to-all-start = ((bf16[16,256,448]{1,2,0:T(8,128)(2,1)}), bf16[16,256,448]{1,2,0:T(8,128)(2,1)}, u32[]{:S(2)}, u32[]{:S(2)}) async-start(bf16[16,256,448]{1,2,0:T(8,128)(2,1)} %stack.2), calls=%async_computation | async-start | bytes 7340032 | tf_op jit(solution)/shard_map/all_to_all | solution.py:20
  17.4 0.0 all-gather.2.cloned.1.call-start
  17.4 0.0 copy-done.1
  17.5 62.3 %all_gather.6 = s32[4096,2]{0,1:T(2,128)S(1)} all-gather(s32[256,2]{0,1:T(2,128)S(1)} %copy-done.1), channel_id=1, replica_groups=mesh['expert'=16,'hidden'=16] {'expert'}, dimensions={0}, use_global_device_ids=true | all-gather | bytes 34816 | tf_op jit(solution)/shard_map/all_gather | solution.py:22
  79.8 0.6 reduce-window.16
  80.4 0.2 slice_reduce_fusion
  80.6 0.1 bitcast_subtract_fusion
  80.7 0.0 all-to-all-done
  80.7 3.2 convolution_convert_fusion
  83.9 1.1 copy.29
  84.9 0.0 all-gather.2.cloned.1.call-update
  85.0 0.0 reduce-scatter.2.cloned.1.call-start
  85.0 143.0 %all-gather.2.cloned.1.call-done = bf16[640,7168]{0,1:T(8,128)(2,1)} async-done(((bf16[640,448]{0,1:T(8,128)(2,1)}), bf16[640,7168]{0,1:T(8,128)(2,1)}) %all-gather.2.cloned.1.call-update) | async-done | bytes 9175056 | tf_op jit(solution)/shard_map/all_gather | solution.py:39
  228.1 6.7 %fusion.4 = f32[640,128]{1,0:T(8,128)S(1)} fusion(bf16[640,7168]{0,1:T(8,128)(2,1)} %all-gather.2.cloned.1.call-done, bf16[1,7168,128]{2,1,0:T(8,128)(2,1)} %param.9), kind=kOutput, calls=%fused_computation.4 | convolution fusion | flops 1174405120 | bytes 11337728 | tf_op jit(solution)/shard_map/dot_general | solution.py:40
  234.7 0.0 copy-done
  234.8 20.0 %fusion = f32[640,7168]{0,1:T(8,128)} fusion(bf16[1,128,7168]{2,1,0:T(8,128)(2,1)S(1)} %copy-done, bf16[640,7168]{0,1:T(8,128)(2,1)} %all-gather.2.cloned.1.call-done, bf16[1,7168,128]{2,1,0:T(8,128)(2,1)} %param.10, f32[640,128]{1,0:T(8,128)S(1)} %fusion.4), kind=kOutput, calls=%fused_computation | convolution fusion | flops 2349301760 | bytes 31522816 | tf_op jit(solution)/shard_map/dot_general | solution.py:43
  254.8 0.0 reduce-scatter.2.cloned.1.call-update
  254.8 0.0 copy-start.2
  254.9 0.6 reduce-window.14
  255.4 0.2 slice_reduce_fusion.1
  255.7 302.8 %reduce-scatter.2.cloned.1.call-done = f32[640,448]{0,1:T(8,128)} async-done(((f32[640,7168]{0,1:T(8,128)}), f32[640,448]{0,1:T(8,128)}) %reduce-scatter.2.cloned.1.call-update) | async-done | bytes 1146896 | tf_op jit(solution)/shard_map/reduce_scatter | solution.py:44
  558.4 1.3 convert_element_type.25
  559.8 1.1 copy.30
  560.9 5.5 all-to-all-start.1
  566.4 0.0 copy-done.2
  566.4 0.1 bitcast_subtract_fusion.1
  566.5 11.1 %all-to-all-done.1 = bf16[16,40,448]{2,1,0:T(8,128)(2,1)S(1)} async-done(((bf16[16,40,448]{2,1,0:T(8,128)(2,1)}), bf16[16,40,448]{2,1,0:T(8,128)(2,1)S(1)}, u32[]{:S(2)}, u32[]{:S(2)}) %all-to-all-start.1) | async-done | bytes 573472 | tf_op jit(solution)/shard_map/all_to_all | solution.py:46
  577.7 1.7 fusion.6
  (12 shorter events, 0.2 us)
Async XLA Ops:
  6.5 228.2 %copy-start = (bf16[1,128,7168]{2,1,0:T(8,128)(2,1)S(1)}, bf16[1,128,7168]{2,1,0:T(8,128)(2,1)}, u32[]{:S(2)}) copy-start(bf16[1,128,7168]{2,1,0:T(8,128)(2,1)} %param.11) | copy-start | bytes 5505028
  9.8 7.7 %copy-start.1 = (s32[256,2]{0,1:T(2,128)S(1)}, s32[256,2]{0,1:T(2,128)}, u32[]{:S(2)}) copy-start(s32[256,2]{0,1:T(2,128)} %param.7) | copy-start | bytes 6148
  9.8 70.9 %all-to-all-start = ((bf16[16,256,448]{1,2,0:T(8,128)(2,1)}), bf16[16,256,448]{1,2,0:T(8,128)(2,1)}, u32[]{:S(2)}, u32[]{:S(2)}) async-start(bf16[16,256,448]{1,2,0:T(8,128)(2,1)} %stack.2), calls=%async_computation | async-start | bytes 7340032 | tf_op jit(solution)/shard_map/all_to_all | solution.py:20
  17.4 210.7 %all-gather.2.cloned.1.call-start = ((), (), s32[]{:S(2)}) async-start(), calls=%async_computation.3 | async-start | bytes 9748480 | tf_op jit(solution)/shard_map/all_gather | solution.py:39
  85.0 473.5 %reduce-scatter.2.cloned.1.call-start = ((), (), s32[]{:S(2)}) async-start(), calls=%async_computation.4 | async-start | bytes 19496960 | tf_op jit(solution)/shard_map/reduce_scatter | solution.py:44
  254.8 311.6 %copy-start.2 = (f32[256,2]{0,1:T(2,128)S(1)}, f32[256,2]{0,1:T(2,128)}, u32[]{:S(2)}) copy-start(f32[256,2]{0,1:T(2,128)} %param.8) | copy-start | bytes 6148
  560.9 16.8 %all-to-all-start.1 = ((bf16[16,40,448]{2,1,0:T(8,128)(2,1)}), bf16[16,40,448]{2,1,0:T(8,128)(2,1)S(1)}, u32[]{:S(2)}, u32[]{:S(2)}) async-start(bf16[16,40,448]{2,1,0:T(8,128)(2,1)} %bitcast.7), calls=%async_computation.2 | async-start | bytes 1310720 | tf_op jit(solution)/shard_map/all_to_all | solution.py:46
Sparse Core Ops, SparseCore 0:
  85.1 142.9 all-gather.1
  254.9 303.4 reduce-scatter.1
